TPU v7x, 32 devices: a whole 2x2x4 slice. The times are simulated.
32 devices in a mesh: groups: 2 (over y), patch: 4 (over z), rows: 4 (over x, core).
Axes of the slice: x: 2, y: 2, z: 4, core: 2. Of those that a mesh axis runs over, the one named last changes fastest.
Arguments:
- panel: bfloat16 [2, 16384, 256], P(None, ('groups', 'patch', 'rows')), parts along dimension 1, may hold values from -6 to 6
- pairing: float32 [16384], P(('groups', 'patch', 'rows')), parts along dimension 0, may hold values from 0.1 to 0.5
- hop_blocks: bfloat16 [128, 8, 128, 128], P(('groups', 'patch', 'rows')), parts along dimension 0, may hold values from -0.09375 to 0.09375
- hop_cols: int32 [128, 8], P(('groups', 'patch', 'rows')), parts along dimension 0, may hold values from 0 to 15
- bnd_weight: bfloat16 [4096, 512], P(('groups', 'patch', 'rows')), parts along dimension 0, may hold values from -0.125 to 0.125
- attract: float32 [64], replicated, may hold values from 4 to 16
- attract_class: int32 [16384], P(('groups', 'patch', 'rows')), parts along dimension 0, may hold values from 0 to 63
- target: float32 [16384], P(('groups', 'patch', 'rows')), parts along dimension 0, may hold values from -6 to 6
Outputs:
- cheb_two: bfloat16 [2, 16384, 256], P(None, ('groups', 'patch', 'rows')), parts along dimension 1
- new_pair: float32 [16384], P(('groups', 'patch', 'rows')), parts along dimension 0
- class_grad: float32 [8, 64], P(('groups', 'patch'), 'rows'), parts along dimension 0
There are 2 independent parts, one for each index of `groups`. A program takes and returns all parts, laid end to end along the dimension named above; an argument that names none is the same for every part. Nothing has to cross between parts.
Inputs may be any that keep to these rules, and one draw needn't show every extreme that they name: `hop_cols`: entries of a block row may repeat.
All inputs are finite; a program needn't handle non-finite values.
Results may differ from a plain program's by a relative error of at most 0.0044.
Values may be sent and summed in bfloat16 or wider, within the bound.
A program may use at most 64 MiB of HBM per device.

v0:
```python
import jax
import jax.numpy as jnp
from jax import lax
from jax.sharding import PartitionSpec as P

coef_zero = 0.5
coef_one = 0.55
coef_two = -0.3


def shifted(block, axis, distance):
    devices = range(lax.axis_size(axis))
    route = [((i - distance) % len(devices), i) for i in devices]
    return lax.ppermute(block, axis, route)


def neighbour_sites(panel, edge_rows):
    slab = panel[:, :edge_rows]
    offsets = [-1, 1, -2, 2]
    pieces = []
    for offset in offsets:
        pieces.append(shifted(slab, "patch", -offset))
    return jnp.concatenate(pieces, axis=1)


def bdg_apply(panel, pairing, hop_blocks, hop_cols, bnd_weight):
    width = panel.shape[2]
    local_rows = panel.shape[1]
    edge_rows = bnd_weight.shape[0]
    whole = lax.all_gather(panel, "rows", axis=1, tiled=True)
    pblocks = whole.shape[1] // 128
    picked = jnp.take(whole.reshape(2, pblocks, 128, width), hop_cols, axis=1)
    inner = jnp.einsum("bnrs,cbnsk->cbrk", hop_blocks, picked, preferred_element_type=jnp.float32)
    inner = inner.reshape(2, local_rows, width)
    near = neighbour_sites(panel, edge_rows)
    edge = jnp.einsum("ij,cjk->cik", bnd_weight, near, preferred_element_type=jnp.float32)
    hopped = jnp.concatenate([inner[:, :edge_rows] + edge, inner[:, edge_rows:]], axis=1)
    values = panel.astype(jnp.float32)
    particle = hopped[0] + pairing[:, None] * values[1]
    hole = pairing[:, None] * values[0] - hopped[1]
    return jnp.stack([particle, hole])


def on_device(panel, pairing, hop_blocks, hop_cols, bnd_weight, attract, attract_class, target):
    width = panel.shape[2]
    first = bdg_apply(panel, pairing, hop_blocks, hop_cols, bnd_weight).astype(jnp.bfloat16)
    second = 2.0 * bdg_apply(first, pairing, hop_blocks, hop_cols, bnd_weight) - panel.astype(
        jnp.float32
    )
    cheb_two = second.astype(jnp.bfloat16)
    values = panel.astype(jnp.float32)
    moment = coef_zero * values[0] + coef_one * first[0].astype(jnp.float32) + coef_two * second[0]
    gvalue = jnp.sum(values[1] * moment, axis=1) / width
    classes = attract.shape[0]
    onehot = (attract_class[:, None] == jnp.arange(classes, dtype=jnp.int32)[None, :]).astype(
        jnp.float32
    )
    gain = jnp.dot(onehot, attract, precision=lax.Precision.HIGHEST)
    new_pair = gain * gvalue
    class_terms = jnp.dot(target * gvalue, onehot, precision=lax.Precision.HIGHEST).reshape(
        1, classes
    )
    class_grad = lax.psum_scatter(class_terms, "rows", scatter_dimension=1, tiled=True)
    return (cheb_two, new_pair, class_grad)


def solution(mesh):
    return jax.shard_map(
        on_device,
        mesh=mesh,
        in_specs=(
            P(None, ("groups", "patch", "rows"), None),
            P(("groups", "patch", "rows")),
            P(("groups", "patch", "rows"), None, None, None),
            P(("groups", "patch", "rows"), None),
            P(("groups", "patch", "rows"), None),
            P(),
            P(("groups", "patch", "rows")),
            P(("groups", "patch", "rows")),
        ),
        out_specs=(
            P(None, ("groups", "patch", "rows"), None),
            P(("groups", "patch", "rows")),
            P(("groups", "patch"), "rows"),
        ),
        check_vma=False,
    )
```

profile of v0, /device:TPU:0, one launch (start us, length us, event | category | flops | bytes accessed | tf_op | source)
XLA Modules:
  0.0 107.3 jit_solution(15779433388095788398)
XLA Ops:
  7.2 0.0 copy-start
  7.2 0.0 all-gather.3.cloned.1.call-start
  7.2 0.7 all-gather.3.cloned.1.call-update
  7.9 0.0 all-gather.5.cloned.1.call-start
  8.0 0.9 slice.51
  8.9 3.1 %collective-permute-start = (bf16[2,128,256]{2,1,0:T(8,128)(2,1)S(1)}, bf16[2,128,256]{2,1,0:T(8,128)(2,1)S(1)}, u32[]{:S(2)}, u32[]{:S(2)}) collective-permute-start(bf16[2,128,256]{2,1,0:T(8,128)(2,1)S(1)} %slice.51), channel_id=1, source_target_pairs={{12,0},{0,4},{4,8},{8,12},{13,1},{1,5},{5,9},{9,13},{14,2},{2,6},{... | collective-permute-start | bytes 393224 | tf_op jit(solution)/shard_map/ppermute | solution.py:14
  12.0 2.1 %collective-permute-start.1 = (bf16[2,128,256]{2,1,0:T(8,128)(2,1)S(1)}, bf16[2,128,256]{2,1,0:T(8,128)(2,1)S(1)}, u32[]{:S(2)}, u32[]{:S(2)}) collective-permute-start(bf16[2,128,256]{2,1,0:T(8,128)(2,1)S(1)} %slice.51), channel_id=1, source_target_pairs={{4,0},{8,4},{12,8},{0,12},{5,1},{9,5},{13,9},{1,13},{6,2},{10,6},{... | collective-permute-start | bytes 393224 | tf_op jit(solution)/shard_map/ppermute | solution.py:14
  14.0 0.9 collective-permute-start.2
  15.0 1.1 %convert_element_type.17 = f32[2,512,256]{2,1,0:T(8,128)S(1)} convert(bf16[2,512,256]{2,1,0:T(8,128)(2,1)} %param.10) | non-fusion elementwise | flops 262144 | bytes 1572864 | tf_op jit(solution)/shard_map/convert_element_type | solution.py:38
  16.1 0.7 compare_select_fusion
  16.8 0.1 reshape.80
  16.9 0.7 compare_and_fusion
  17.6 17.3 %all-gather.3.cloned.1.call-done = bf16[2,2048,256]{2,1,0:T(8,128)(2,1)} async-done(((bf16[2,512,256]{2,1,0:T(8,128)(2,1)}), bf16[2,2048,256]{2,1,0:T(8,128)(2,1)}) %all-gather.3.cloned.1.call-update) | async-done | bytes 2097168 | tf_op jit(solution)/shard_map/all_gather | solution.py:30
  34.9 4.4 %gather_fusion = bf16[32,2,128,256]{3,2,1,0:T(8,128)(2,1)} fusion(bf16[2,16,128,256]{3,2,1,0:T(8,128)(2,1)} %bitcast.63, s32[1024]{0:T(1024)S(1)} %pad_clamp_fusion), kind=kCustom, calls=%fused_computation.clone | custom fusion | bytes 8388736 | tf_op jit(solution)/shard_map/jit(_take)/gather | solution.py:32
  39.2 0.0 copy-done
  39.2 3.2 %fusion.10 = f32[2,4,128,256]{3,2,0,1:T(8,128)S(1)} fusion(bf16[4,8,2,128,256]{4,3,2,1,0:T(8,128)(2,1)} %bitcast.66, pred[4,8]{1,0:T(4,128)(4,1)S(1)} %compare_and_fusion, bf16[4,8,128,128]{3,2,1,0:T(8,128)(2,1)S(1)} %copy-done), kind=kOutput, calls=%fused_computation.12 | convolution fusion | flops 538968064 | bytes 6291488 | tf_op jit(solution)/shard_map/bnrs,cbnsk->cbrk/dot_general | solution.py:33
  42.5 0.0 copy-start.3
  42.5 0.1 copy.20
  42.6 0.0 copy-start.7
  42.6 0.0 copy-start.9
  42.6 0.1 slice.71
  42.7 0.0 collective-permute-done
  42.7 0.0 collective-permute-done.1
  42.7 0.0 collective-permute-done.2
  42.7 0.0 copy-done.5
  42.7 0.2 fusion.17
  43.0 0.2 copy-done.3
  43.1 0.2 fusion.25
  43.3 0.0 copy-start.2
  43.3 0.7 copy-done.2
  44.0 0.9 fusion.57
  44.9 0.0 all-gather.5.cloned.1.call-update
  45.0 0.0 reduce-scatter.4.cloned.1.call-start
  45.0 0.0 copy-done.7
  45.0 0.0 copy-done.9
  45.0 0.3 fusion.46
  45.3 0.9 fusion.47
  46.2 1.5 %collective-permute-start.3 = (bf16[2,128,256]{2,1,0:T(8,128)(2,1)S(1)}, bf16[2,128,256]{2,1,0:T(8,128)(2,1)}, u32[]{:S(2)}, u32[]{:S(2)}) collective-permute-start(bf16[2,128,256]{2,1,0:T(8,128)(2,1)S(1)} %fusion.47), channel_id=1, source_target_pairs={{12,0},{0,4},{4,8},{8,12},{13,1},{1,5},{5,9},{9,13},{14,2},{2,6},{... | collective-permute-start | bytes 393224 | tf_op jit(solution)/shard_map/ppermute | solution.py:14
  47.8 2.3 %collective-permute-start.4 = (bf16[2,128,256]{2,1,0:T(8,128)(2,1)S(1)}, bf16[2,128,256]{2,1,0:T(8,128)(2,1)}, u32[]{:S(2)}, u32[]{:S(2)}) collective-permute-start(bf16[2,128,256]{2,1,0:T(8,128)(2,1)S(1)} %fusion.47), channel_id=1, source_target_pairs={{4,0},{8,4},{12,8},{0,12},{5,1},{9,5},{13,9},{1,13},{6,2},{10,6},{... | collective-permute-start | bytes 393224 | tf_op jit(solution)/shard_map/ppermute | solution.py:14
  50.1 0.6 collective-permute-start.5
  50.7 17.0 %all-gather.5.cloned.1.call-done = bf16[2,2048,256]{2,1,0:T(8,128)(2,1)} async-done(((bf16[2,512,256]{2,1,0:T(8,128)(2,1)}), bf16[2,2048,256]{2,1,0:T(8,128)(2,1)}) %all-gather.5.cloned.1.call-update) | async-done | bytes 2097168 | tf_op jit(solution)/shard_map/all_gather | solution.py:30
  67.7 4.4 %gather_fusion.1 = bf16[32,2,128,256]{3,2,1,0:T(8,128)(2,1)} fusion(bf16[2,16,128,256]{3,2,1,0:T(8,128)(2,1)} %bitcast.64, s32[1024]{0:T(1024)S(1)} %pad_clamp_fusion), kind=kCustom, calls=%fused_computation.1.clone | custom fusion | bytes 8388736 | tf_op jit(solution)/shard_map/jit(_take)/gather | solution.py:32
  72.1 3.2 %fusion.13 = f32[2,4,128,256]{3,2,0,1:T(8,128)S(1)} fusion(bf16[4,8,2,128,256]{4,3,2,1,0:T(8,128)(2,1)} %bitcast.65, pred[4,8]{1,0:T(4,128)(4,1)S(1)} %compare_and_fusion, bf16[4,8,128,128]{3,2,1,0:T(8,128)(2,1)S(1)} %copy-done), kind=kOutput, calls=%fused_computation.13 | convolution fusion | flops 538968064 | bytes 6291488 | tf_op jit(solution)/shard_map/bnrs,cbnsk->cbrk/dot_general | solution.py:33
  75.3 0.0 copy-start.1
  75.3 0.1 copy.22
  75.4 0.1 slice.79
  75.5 0.0 collective-permute-done.3
  75.5 0.0 collective-permute-done.4
  75.5 0.0 collective-permute-done.5
  75.5 0.0 copy-done.6
  75.5 1.3 %fusion.16 = f32[2,128,256]{2,1,0:T(8,128)S(1)} fusion(bf16[2,128,256]{2,1,0:T(8,128)(2,1)} %collective-permute-done.5, bf16[2,128,256]{2,1,0:T(8,128)(2,1)} %collective-permute-done.4, bf16[2,128,256]{2,1,0:T(8,128)(2,1)} %collective-permute-done.3, f32[2,512,256]{2,1,0:T(8,128)S(1)} %bitcast.70, bf16[128,512]{1,0:T(8,128)(2,1)S(1)} %copy-done.6), kind=kOutput, calls=%fused_computation.15 | convolution fusion | flops 69271552 | bytes 1048576 | tf_op jit(solution)/shard_map/ij,cjk->cik/dot_general | solution.py:36
  76.8 0.0 copy-start.4
  76.9 0.0 copy-start.8
  76.9 0.2 fusion.22
  77.1 0.0 copy-done.1
  77.1 1.0 fusion.58
  78.0 0.2 fusion.28
  78.2 0.0 copy-done.4
  78.2 0.6 multiply_multiply_fusion
  78.8 0.0 copy-done.8
  78.8 1.1 %convolution_bitcast_fusion.2 = f32[64,1]{1,0:T(8,128)} fusion(f32[512,1]{0,1:T(1,128)S(1)} %bitcast.73, s32[512]{0:T(512)S(1)} %copy-done.8), kind=kOutput, calls=%fused_computation.18 | convolution fusion | flops 425984 | bytes 4352
  79.9 0.0 reduce-scatter.4.cloned.1.call-update
  79.9 19.5 %reduce-scatter.4.cloned.1.call-done = f32[16,1]{1,0:T(8,128)} async-done(((f32[64,1]{1,0:T(8,128)}), f32[16,1]{1,0:T(8,128)}) %reduce-scatter.4.cloned.1.call-update) | async-done | bytes 80
  99.5 1.3 %copy.27 = f32[1,16]{1,0:T(1,128)} copy(f32[1,16]{0,1:T(8,128)} %bitcast.71) | data formatting | bytes 128
  (3 shorter events, 0.0 us)
Async XLA Ops:
  7.2 32.1 %copy-start = (bf16[4,8,128,128]{3,2,1,0:T(8,128)(2,1)S(1)}, bf16[4,8,128,128]{3,2,1,0:T(8,128)(2,1)}, u32[]{:S(2)}) copy-start(bf16[4,8,128,128]{3,2,1,0:T(8,128)(2,1)} %param.12) | copy-start | bytes 3145732
  7.2 27.7 %all-gather.3.cloned.1.call-start = ((), (), s32[]{:S(2)}) async-start(), calls=%async_computation.1 | async-start | bytes 2621440 | tf_op jit(solution)/shard_map/all_gather | solution.py:30
  7.9 59.8 %all-gather.5.cloned.1.call-start = ((), (), s32[]{:S(2)}) async-start(), calls=%async_computation.2 | async-start | bytes 2621440 | tf_op jit(solution)/shard_map/all_gather | solution.py:30
  8.9 33.8 %collective-permute-start = (bf16[2,128,256]{2,1,0:T(8,128)(2,1)S(1)}, bf16[2,128,256]{2,1,0:T(8,128)(2,1)S(1)}, u32[]{:S(2)}, u32[]{:S(2)}) collective-permute-start(bf16[2,128,256]{2,1,0:T(8,128)(2,1)S(1)} %slice.51), channel_id=1, source_target_pairs={{12,0},{0,4},{4,8},{8,12},{13,1},{1,5},{5,9},{9,13},{14,2},{2,6},{... | collective-permute-start | bytes 393224 | tf_op jit(solution)/shard_map/ppermute | solution.py:14
  12.0 30.7 %collective-permute-start.1 = (bf16[2,128,256]{2,1,0:T(8,128)(2,1)S(1)}, bf16[2,128,256]{2,1,0:T(8,128)(2,1)S(1)}, u32[]{:S(2)}, u32[]{:S(2)}) collective-permute-start(bf16[2,128,256]{2,1,0:T(8,128)(2,1)S(1)} %slice.51), channel_id=1, source_target_pairs={{4,0},{8,4},{12,8},{0,12},{5,1},{9,5},{13,9},{1,13},{6,2},{10,6},{... | collective-permute-start | bytes 393224 | tf_op jit(solution)/shard_map/ppermute | solution.py:14
  14.0 28.6 %collective-permute-start.2 = (bf16[2,128,256]{2,1,0:T(8,128)(2,1)S(1)}, bf16[2,128,256]{2,1,0:T(8,128)(2,1)S(1)}, u32[]{:S(2)}, u32[]{:S(2)}) collective-permute-start(bf16[2,128,256]{2,1,0:T(8,128)(2,1)S(1)} %slice.51), channel_id=1, source_target_pairs={{8,0},{12,4},{0,8},{4,12},{9,1},{13,5},{1,9},{5,13},{10,2},{14,6},... | collective-permute-start | bytes 393224 | tf_op jit(solution)/shard_map/ppermute | solution.py:14
  39.2 3.5 %copy-start.5 = (bf16[128,512]{1,0:T(8,128)(2,1)S(1)}, bf16[128,512]{1,0:T(8,128)(2,1)}, u32[]{:S(2)}) copy-start(bf16[128,512]{1,0:T(8,128)(2,1)} %param.14) | copy-start | bytes 393220
  42.5 0.7 copy-start.3
  42.6 2.4 %copy-start.7 = (s32[512]{0:T(512)S(1)}, s32[512]{0:T(512)}, u32[]{:S(2)}) copy-start(s32[512]{0:T(512)} %param.16) | copy-start | bytes 6148
  42.6 2.4 %copy-start.9 = (f32[64]{0:T(128)S(1)}, f32[64]{0:T(128)}, u32[]{:S(2)}) copy-start(f32[64]{0:T(128)} %param.15) | copy-start | bytes 772
  43.3 0.7 copy-start.2
  45.0 54.5 %reduce-scatter.4.cloned.1.call-start = ((), (), s32[]{:S(2)}) async-start(), calls=%async_computation.3 | async-start | bytes 40960
  46.2 29.2 %collective-permute-start.3 = (bf16[2,128,256]{2,1,0:T(8,128)(2,1)S(1)}, bf16[2,128,256]{2,1,0:T(8,128)(2,1)}, u32[]{:S(2)}, u32[]{:S(2)}) collective-permute-start(bf16[2,128,256]{2,1,0:T(8,128)(2,1)S(1)} %fusion.47), channel_id=1, source_target_pairs={{12,0},{0,4},{4,8},{8,12},{13,1},{1,5},{5,9},{9,13},{14,2},{2,6},{... | collective-permute-start | bytes 393224 | tf_op jit(solution)/shard_map/ppermute | solution.py:14
  47.8 27.7 %collective-permute-start.4 = (bf16[2,128,256]{2,1,0:T(8,128)(2,1)S(1)}, bf16[2,128,256]{2,1,0:T(8,128)(2,1)}, u32[]{:S(2)}, u32[]{:S(2)}) collective-permute-start(bf16[2,128,256]{2,1,0:T(8,128)(2,1)S(1)} %fusion.47), channel_id=1, source_target_pairs={{4,0},{8,4},{12,8},{0,12},{5,1},{9,5},{13,9},{1,13},{6,2},{10,6},{... | collective-permute-start | bytes 393224 | tf_op jit(solution)/shard_map/ppermute | solution.py:14
  50.1 25.4 %collective-permute-start.5 = (bf16[2,128,256]{2,1,0:T(8,128)(2,1)S(1)}, bf16[2,128,256]{2,1,0:T(8,128)(2,1)}, u32[]{:S(2)}, u32[]{:S(2)}) collective-permute-start(bf16[2,128,256]{2,1,0:T(8,128)(2,1)S(1)} %fusion.47), channel_id=1, source_target_pairs={{8,0},{12,4},{0,8},{4,12},{9,1},{13,5},{1,9},{5,13},{10,2},{14,6},... | collective-permute-start | bytes 393224 | tf_op jit(solution)/shard_map/ppermute | solution.py:14
  72.1 3.4 %copy-start.6 = (bf16[128,512]{1,0:T(8,128)(2,1)S(1)}, bf16[128,512]{1,0:T(8,128)(2,1)}, u32[]{:S(2)}) copy-start(bf16[128,512]{1,0:T(8,128)(2,1)} %param.14) | copy-start | bytes 393220
  75.3 1.8 %copy-start.1 = (bf16[2,512,256]{2,1,0:T(8,128)(2,1)S(1)}, bf16[2,512,256]{2,1,0:T(8,128)(2,1)}, u32[]{:S(2)}) copy-start(bf16[2,512,256]{2,1,0:T(8,128)(2,1)} %param.10) | copy-start | bytes 1572868
  76.8 1.4 %copy-start.4 = (f32[512]{0:T(512)S(1)}, f32[512]{0:T(512)}, u32[]{:S(2)}) copy-start(f32[512]{0:T(512)} %param.17) | copy-start | bytes 6148
  76.9 2.0 %copy-start.8 = (s32[512]{0:T(512)S(1)}, s32[512]{0:T(512)}, u32[]{:S(2)}) copy-start(s32[512]{0:T(512)} %param.16) | copy-start | bytes 6148
Sparse Core Ops, SparseCore 0:
  9.6 25.2 all-gather.2
  45.1 22.5 all-gather.4
  80.0 19.3 reduce-scatter.3
where the time goes:
time: 108 us; the launch traced here: 107 us
  waiting for transfers between devices  54.6 us (51%)
  between operations  14 us (13%)
  local copies, waits for them, and re-layouts  12.3 us (11%)
  starting transfers between devices  10.7 us (10%)
  matrix products  9.36 us (9%)
  other arithmetic  6.37 us (6%)
    all_gather x2, waiting for transfers between devices, bdg_apply(): whole = lax.all_gather(panel, 'rows', axis=1, tiled=True)  34.3 us
    unnamed x4, waiting for transfers between devices  20.2 us
    ppermute x6, starting transfers between devices, shifted(): return lax.ppermute(block, axis, route)  10.6 us
    gather x2, local copies, waits for them, and re-layouts, bdg_apply(): picked = jnp.take(whole.reshape(2, pblocks, 128, width), hop_cols, axis=1)  8.7 us
    dot_general x2, matrix products, bdg_apply(): jnp.einsum('bnrs,cbnsk->cbrk', hop_blocks, picked, preferred_element_type...  6.4 us
    unnamed x21, local copies, waits for them, and re-layouts  2.23 us
  transfers between devices with their start and end apart: 9, of which 3 were waited for; matrix products, arithmetic and copies ran while one was open for 19% of the time, Pallas kernels for 0%

commit v1 on v0

v1 whole, which is shorter than its diff:
```python
import functools

import jax
import jax.numpy as jnp
from jax import lax
from jax.experimental import pallas as pl
from jax.experimental.pallas import tpu as pltpu
from jax.sharding import PartitionSpec as P

coef_zero = 0.5
coef_one = 0.55
coef_two = -0.3

LANES = 128
BLOCK = 128
OFFSETS = (-1, 1, -2, 2)
MESH = pl.DeviceIdType.MESH
HIGHEST = lax.Precision.HIGHEST
LANE_DIMS = (((1,), (1,)), ((), ()))


def distinct(n_patch):
    shifts = []
    for offset in OFFSETS:
        if offset % n_patch not in shifts:
            shifts.append(offset % n_patch)
    return shifts


def kernel(
    n_rows, n_patch,
    cols_ref, pairing_ref, bnd_ref, attract_ref, class_ref, target_ref, panel_ref, hop_ref,
    cheb_ref, pair_out_ref, grad_ref,
    pbufs, fbufs, pnear, fnear, outs, hop, pair, moments, terms,
    peer_send, peer_recv, mate_send, mate_recv, fwd_send, fwd_recv,
    near_send, near_recv, term_send, term_recv, load_sem, hop_sem, store_sem,
):
    n_blocks = panel_ref.shape[1]
    rows = n_blocks * BLOCK
    width = panel_ref.shape[3]
    edge = bnd_ref.shape[0]
    edge_blocks = edge // BLOCK
    classes = attract_ref.shape[1]
    n_links = hop_ref.shape[1]
    halves = width // LANES
    shifts = distinct(n_patch)
    chunks = [(c, k) for c in range(2) for k in range(halves)]
    n_chunks = len(chunks)
    n_peers = n_rows // 2 - 1

    me = lax.axis_index("rows")
    patch = lax.axis_index("patch")
    mate = me + 1 - 2 * lax.rem(me, 2)

    def row_id(distance):
        return lax.rem(me + distance, n_rows)

    def span(owner):
        return pl.ds(owner * n_blocks, n_blocks)

    def patch_id(shift):
        return lax.rem(patch + shift, n_patch)

    barrier = pltpu.get_barrier_semaphore()
    for distance in range(1, n_rows):
        pl.semaphore_signal(barrier, inc=1, device_id={"rows": row_id(distance)}, device_id_type=MESH)
    for shift in shifts:
        pl.semaphore_signal(barrier, inc=1, device_id={"patch": patch_id(shift)}, device_id_type=MESH)

    hop_copy = pltpu.make_async_copy(hop_ref, hop, hop_sem)
    loads = []
    for i, (c, k) in enumerate(chunks):
        lanes = pl.ds(k * LANES, LANES)
        loads.append(
            pltpu.make_async_copy(panel_ref.at[c, :, :, lanes], pbufs[i].at[span(me)], load_sem.at[i])
        )
        loads[i].start()
    hop_copy.start()
    pl.semaphore_wait(barrier, n_rows - 1 + len(shifts))

    def sends(step, own, slab, dest, near):
        peers = [
            pltpu.make_async_remote_copy(
                own, dest.at[span(me)], peer_send.at[step, j], peer_recv.at[step, j],
                device_id={"rows": row_id(n_rows - 2 * (j + 1))}, device_id_type=MESH,
            )
            for j in range(n_peers)
        ]
        to_mate = pltpu.make_async_remote_copy(
            own, dest.at[span(me)], mate_send.at[step], mate_recv.at[step],
            device_id={"rows": mate}, device_id_type=MESH,
        )
        to_near = [
            pltpu.make_async_remote_copy(
                slab, near.at[pl.ds(j * edge_blocks, edge_blocks)], near_send.at[step, j], near_recv.at[step, j],
                device_id={"patch": patch_id(n_patch - shift)}, device_id_type=MESH,
            )
            for j, shift in enumerate(shifts)
        ]
        forwards = []
        for j in range(n_peers):
            block = dest.at[span(row_id(2 * (j + 1)))]
            forwards.append(
                pltpu.make_async_remote_copy(
                    block, block, fwd_send.at[step, j], fwd_recv.at[step, j],
                    device_id={"rows": mate}, device_id_type=MESH,
                )
            )
        return peers, to_mate, to_near, forwards

    def launch(copies):
        peers, to_mate, to_near, _ = copies
        for copy in peers + to_near + [to_mate]:
            copy.start()

    def arrive(copies):
        peers, to_mate, to_near, forwards = copies
        for peer, forward in zip(peers, forwards):
            peer.wait_recv()
            forward.start()
        to_mate.wait_recv()
        for copy in to_near:
            copy.wait_recv()
        for forward in forwards:
            forward.wait_recv()

    def hopped(buf, near, b):
        left = [hop[b, n] for n in range(n_links)]
        right = [buf[cols_ref[b, n]] for n in range(n_links)]
        if b * BLOCK < edge:
            left.append(bnd_ref[pl.ds(b * BLOCK, BLOCK), :])
            for offset in OFFSETS:
                slot = shifts.index(offset % n_patch) * edge_blocks
                right.extend(near[slot + e] for e in range(edge_blocks))
        return jnp.dot(
            jnp.concatenate(left, axis=1),
            jnp.concatenate(right, axis=0),
            preferred_element_type=jnp.float32,
        )

    started = []
    for i, (c, k) in enumerate(chunks):
        lanes = pl.ds(k * LANES, LANES)
        started.append(
            sends(i, panel_ref.at[c, :, :, lanes], panel_ref.at[c, pl.ds(0, edge_blocks), :, lanes], pbufs[i], pnear[i])
        )
        launch(started[i])

    for b in range(rows // BLOCK):
        sites = pl.ds(b * BLOCK, BLOCK)
        wide = jnp.broadcast_to(pairing_ref[:, sites], (BLOCK, BLOCK))
        pair[sites, :] = wide.T

    hop_copy.wait()
    for i in range(n_chunks):
        loads[i].wait()

    for i, (c, k) in enumerate(chunks):
        arrive(started[i])
        other = (1 - c) * halves + k
        for b in range(rows // BLOCK):
            sites = pl.ds(b * BLOCK, BLOCK)
            hv = hopped(pbufs[i], pnear[i], b)
            cross = pair[sites, :] * pbufs[other][me * n_blocks + b].astype(jnp.float32)
            value = cross + hv if c == 0 else cross - hv
            fbufs[i][me * n_blocks + b] = value.astype(jnp.bfloat16)
        started.append(
            sends(
                n_chunks + i, fbufs[i].at[span(me)],
                fbufs[i].at[pl.ds(me * n_blocks, edge_blocks)], fbufs[i], fnear[i],
            )
        )
        launch(started[n_chunks + i])

    term_copies = [
        pltpu.make_async_remote_copy(
            terms.at[0], terms.at[d], term_send.at[d - 1], term_recv.at[d - 1],
            device_id={"rows": row_id(n_rows - d)}, device_id_type=MESH,
        )
        for d in range(1, n_rows)
    ]
    stores = []
    for i, (c, k) in enumerate(chunks):
        arrive(started[n_chunks + i])
        other = (1 - c) * halves + k
        for b in range(rows // BLOCK):
            sites = pl.ds(b * BLOCK, BLOCK)
            mine = me * n_blocks + b
            hv = hopped(fbufs[i], fnear[i], b)
            cross = pair[sites, :] * fbufs[other][mine].astype(jnp.float32)
            before = pbufs[i][mine].astype(jnp.float32)
            second = 2.0 * (cross + hv if c == 0 else cross - hv) - before
            outs[i][b] = second.astype(jnp.bfloat16)
            if c == 0:
                moment = (
                    coef_zero * before
                    + coef_one * fbufs[i][mine].astype(jnp.float32)
                    + coef_two * second
                )
                weighted = pbufs[other][mine].astype(jnp.float32) * moment
                if k == 0:
                    moments[sites, :] = weighted
                else:
                    moments[sites, :] += weighted
        stores.append(
            pltpu.make_async_copy(
                outs[i], cheb_ref.at[c, :, :, pl.ds(k * LANES, LANES)], store_sem.at[i]
            )
        )
        stores[i].start()
        if c == 0 and k == halves - 1:
            ones = jnp.ones((8, LANES), jnp.float32)
            gvalue = lax.dot_general(
                ones, moments[...], LANE_DIMS, precision=HIGHEST,
                preferred_element_type=jnp.float32,
            ) / width
            numbers = lax.broadcasted_iota(jnp.int32, (classes, rows), 0)
            onehot = (numbers == class_ref[...]).astype(jnp.float32)
            gain = jnp.dot(
                jnp.broadcast_to(attract_ref[...], (8, classes)), onehot, precision=HIGHEST,
                preferred_element_type=jnp.float32,
            )
            pair_out_ref[...] = (gain * gvalue)[:1]
            terms[0] = lax.dot_general(
                target_ref[...] * gvalue, onehot, LANE_DIMS, precision=HIGHEST,
                preferred_element_type=jnp.float32,
            )
            for copy in term_copies:
                copy.start()

    for copy in term_copies:
        copy.wait_recv()
    total = terms[0]
    for d in range(1, n_rows):
        total = total + terms[d]
    share = classes // n_rows
    pick = (
        lax.broadcasted_iota(jnp.int32, (classes, share), 0)
        == lax.broadcasted_iota(jnp.int32, (classes, share), 1) + me * share
    ).astype(jnp.float32)
    grad_ref[...] = jnp.dot(
        total, pick, precision=HIGHEST, preferred_element_type=jnp.float32
    )[:1]

    for peers, to_mate, to_near, forwards in started:
        for copy in peers + [to_mate] + to_near + forwards:
            copy.wait_send()
    for copy in term_copies:
        copy.wait_send()
    for copy in stores:
        copy.wait()


def on_device(n_rows, n_patch, panel, pairing, hop_blocks, hop_cols, bnd_weight, attract, attract_class, target):
    _, rows, width = panel.shape
    edge = bnd_weight.shape[0]
    classes = attract.shape[0]
    n_chunks = 2 * (width // LANES)
    n_near = len(distinct(n_patch))
    n_peers = n_rows // 2 - 1
    dma = pltpu.SemaphoreType.DMA
    vmem = pl.BlockSpec(memory_space=pltpu.VMEM)
    anywhere = pl.BlockSpec(memory_space=pl.ANY)

    blocks = rows // BLOCK

    def each(count):
        return [pltpu.VMEM((count, BLOCK, LANES), jnp.bfloat16) for _ in range(n_chunks)]

    cheb_two, new_pair, class_grad = pl.pallas_call(
        functools.partial(kernel, n_rows, n_patch),
        out_shape=(
            jax.ShapeDtypeStruct((2, blocks, BLOCK, width), jnp.bfloat16),
            jax.ShapeDtypeStruct((1, rows), jnp.float32),
            jax.ShapeDtypeStruct((1, classes // n_rows), jnp.float32),
        ),
        in_specs=[pl.BlockSpec(memory_space=pltpu.SMEM)] + [vmem] * 5 + [anywhere] * 2,
        out_specs=(anywhere, vmem, vmem),
        scratch_shapes=[
            each(n_rows * blocks),
            each(n_rows * blocks),
            each(n_near * edge // BLOCK),
            each(n_near * edge // BLOCK),
            each(blocks),
            pltpu.VMEM(hop_blocks.shape, jnp.bfloat16),
            pltpu.VMEM((rows, LANES), jnp.float32),
            pltpu.VMEM((rows, LANES), jnp.float32),
            pltpu.VMEM((n_rows, 8, classes), jnp.float32),
            dma((2 * n_chunks, n_peers)),
            dma((2 * n_chunks, n_peers)),
            dma((2 * n_chunks,)),
            dma((2 * n_chunks,)),
            dma((2 * n_chunks, n_peers)),
            dma((2 * n_chunks, n_peers)),
            dma((2 * n_chunks, n_near)),
            dma((2 * n_chunks, n_near)),
            dma((n_rows - 1,)),
            dma((n_rows - 1,)),
            dma((n_chunks,)),
            dma,
            dma((n_chunks,)),
        ],
        compiler_params=pltpu.CompilerParams(
            collective_id=0, has_side_effects=True, vmem_limit_bytes=56 * 1024 * 1024
        ),
    )(
        hop_cols, pairing.reshape(1, rows), bnd_weight, attract.reshape(1, classes),
        attract_class.reshape(1, rows), target.reshape(1, rows),
        panel.reshape(2, blocks, BLOCK, width), hop_blocks,
    )
    return cheb_two.reshape(panel.shape), new_pair.reshape(rows), class_grad


def solution(mesh):
    return jax.shard_map(
        functools.partial(on_device, mesh.shape["rows"], mesh.shape["patch"]),
        mesh=mesh,
        in_specs=(
            P(None, ("groups", "patch", "rows"), None),
            P(("groups", "patch", "rows")),
            P(("groups", "patch", "rows"), None, None, None),
            P(("groups", "patch", "rows"), None),
            P(("groups", "patch", "rows"), None),
            P(),
            P(("groups", "patch", "rows")),
            P(("groups", "patch", "rows")),
        ),
        out_specs=(
            P(None, ("groups", "patch", "rows"), None),
            P(("groups", "patch", "rows")),
            P(("groups", "patch"), "rows"),
        ),
        check_vma=False,
    )
```

time: 108 us -> 38.2 us (0.35)
  waiting for transfers between devices: 54.6 us -> 0 us
  Pallas kernels: 0 us -> 34.4 us
  between operations: 14 us -> 0.65 us
  starting transfers between devices: 10.7 us -> 0 us
  matrix products: 9.36 us -> 0 us
  local copies, waits for them, and re-layouts: 12.3 us -> 2.98 us
  other arithmetic: 6.37 us -> 0 us
    pallas_call x0 -> x1, Pallas kernels: none -> 34.4 us  [on_device(): pl.pallas_call(functools.partial(kernel, n_rows, n_patch), out_shape=(jax...]
    all_gather x2 -> x0, waiting for transfers between devices: 34.3 us -> none  [bdg_apply(): whole = lax.all_gather(panel, 'rows', axis=1, tiled=True)]
    unnamed x4 -> x0, waiting for transfers between devices: 20.2 us -> none
    ppermute x6 -> x0, starting transfers between devices: 10.6 us -> none  [shifted(): return lax.ppermute(block, axis, route)]
    gather x2 -> x0, local copies, waits for them, and re-layouts: 8.7 us -> none  [bdg_apply(): picked = jnp.take(whole.reshape(2, pblocks, 128, width), hop_cols, axis=1)]
    dot_general x5 -> x0, matrix products: 8.28 us -> none  [the longest x2 6.4 us: bdg_apply(): jnp.einsum('bnrs,cbnsk->cbrk', hop_blocks, picked, preferred_element_type...]
    convert_element_type x3 -> x0, other arithmetic: 2.96 us -> none  [the longest x2 2.01 us: bdg_apply(): values = panel.astype(jnp.float32)]
    unnamed x1 -> x0, matrix products: 1.08 us -> none
  transfers between devices with their start and end apart: 9 -> 0, of which waited for: 3 -> 0; matrix products, arithmetic and copies ran while one was open for 19% -> 0% of each run, Pallas kernels for 0% -> 0%
where the time goes in v1:
time: 38.2 us; the launch traced here: 38.1 us
  Pallas kernels  34.4 us (90%)
  local copies, waits for them, and re-layouts  2.98 us (8%)
  between operations  0.65 us (2%)
    pallas_call x1, Pallas kernels, on_device(): pl.pallas_call(functools.partial(kernel, n_rows, n_patch), out_shape=(jax...  34.4 us
    unnamed x7, local copies, waits for them, and re-layouts  2.98 us

profile of v1, /device:TPU:0, one launch (start us, length us, event | category | flops | bytes accessed | tf_op | source)
XLA Modules:
  0.0 38.1 jit_solution(5658695237174747244)
XLA Ops:
  0.6 34.4 %shard_map.103 = (bf16[2,4,128,256]{3,2,1,0:T(8,128)(2,1)}, f32[1,512]{1,0:T(1,128)}, f32[1,16]{1,0:T(1,128)}) custom-call(s32[4,8]{1,0:T(4,128)} %cols_ref.1, f32[1,512]{1,0:T(1,128)} %bitcast.9, bf16[128,512]{1,0:T(8,128)(2,1)} %bnd_ref.1, f32[1,64]{1,0:T(1,128)} %bitcast.13, s32[1,512]{1,0:T(1,128)} %bitcast.10, f32[1,512]{1,0:T(1,128)} %bitcast.11, ...), custom_call_target="tpu_custom_call" | custom-call | tf_op jit(solution)/shard_map/pallas_call | solution.py:270
  35.1 0.0 copy-start
  35.1 1.9 %copy.14 = bf16[2,512,256]{2,1,0:T(8,128)(2,1)} copy(bf16[2,512,256]{2,1,0:T(8,128)(2,1)} %bitcast.8) | data formatting | bytes 1048576
  37.0 0.0 copy-done
  37.0 0.0 copy-start.1
  37.0 0.6 %copy.15 = f32[512]{0:T(512)} copy(f32[512]{0:T(512)S(1)} %bitcast.12) | data formatting | bytes 4096
  37.5 0.0 copy-done.1
  37.5 0.5 %copy.16 = f32[1,16]{1,0:T(1,128)} copy(f32[1,16]{1,0:T(1,128)S(1)} %copy-done.1) | data formatting | bytes 128
Async XLA Ops:
  35.1 1.9 %copy-start = (f32[1,512]{1,0:T(1,128)S(1)}, f32[1,512]{1,0:T(1,128)}, u32[]{:S(2)}) copy-start(f32[1,512]{1,0:T(1,128)} %get-tuple-element.7) | copy-start | bytes 6148
  37.0 0.6 %copy-start.1 = (f32[1,16]{1,0:T(1,128)S(1)}, f32[1,16]{1,0:T(1,128)}, u32[]{:S(2)}) copy-start(f32[1,16]{1,0:T(1,128)} %get-tuple-element.14) | copy-start | bytes 196

commit v2 on v1

--- a/solution.py
+++ b/solution.py
@@ -29,11 +29,11 @@
 
 def kernel(
     n_rows, n_patch,
-    cols_ref, pairing_ref, bnd_ref, attract_ref, class_ref, target_ref, panel_ref, hop_ref,
+    cols_ref, pairing_ref, bnd_hbm, attract_ref, class_ref, target_ref, panel_ref, hop_ref,
     cheb_ref, pair_out_ref, grad_ref,
-    pbufs, fbufs, pnear, fnear, outs, hop, pair, moments, terms,
+    pbufs, fbufs, pnear, fnear, hop, pair, moments, terms,
     peer_send, peer_recv, mate_send, mate_recv, fwd_send, fwd_recv,
-    near_send, near_recv, term_send, term_recv, load_sem, hop_sem, store_sem,
+    near_send, near_recv, term_send, term_recv, load_sem, hop_sem, bnd_ref, bnd_sem,
 ):
     n_blocks = panel_ref.shape[1]
     rows = n_blocks * BLOCK
@@ -62,11 +62,12 @@
         return lax.rem(patch + shift, n_patch)
 
     barrier = pltpu.get_barrier_semaphore()
+    for shift in reversed(shifts):
+        pl.semaphore_signal(barrier, inc=1, device_id={"patch": patch_id(shift)}, device_id_type=MESH)
     for distance in range(1, n_rows):
         pl.semaphore_signal(barrier, inc=1, device_id={"rows": row_id(distance)}, device_id_type=MESH)
-    for shift in shifts:
-        pl.semaphore_signal(barrier, inc=1, device_id={"patch": patch_id(shift)}, device_id_type=MESH)
-
+
+    bnd_copy = pltpu.make_async_copy(bnd_hbm, bnd_ref, bnd_sem)
     hop_copy = pltpu.make_async_copy(hop_ref, hop, hop_sem)
     loads = []
     for i, (c, k) in enumerate(chunks):
@@ -76,6 +77,7 @@
         )
         loads[i].start()
     hop_copy.start()
+    bnd_copy.start()
     pl.semaphore_wait(barrier, n_rows - 1 + len(shifts))
 
     def sends(step, own, slab, dest, near):
@@ -152,6 +154,7 @@
         pair[sites, :] = wide.T
 
     hop_copy.wait()
+    bnd_copy.wait()
     for i in range(n_chunks):
         loads[i].wait()
 
@@ -179,7 +182,6 @@
         )
         for d in range(1, n_rows)
     ]
-    stores = []
     for i, (c, k) in enumerate(chunks):
         arrive(started[n_chunks + i])
         other = (1 - c) * halves + k
@@ -190,7 +192,7 @@
             cross = pair[sites, :] * fbufs[other][mine].astype(jnp.float32)
             before = pbufs[i][mine].astype(jnp.float32)
             second = 2.0 * (cross + hv if c == 0 else cross - hv) - before
-            outs[i][b] = second.astype(jnp.bfloat16)
+            cheb_ref[c, b, :, pl.ds(k * LANES, LANES)] = second.astype(jnp.bfloat16)
             if c == 0:
                 moment = (
                     coef_zero * before
@@ -202,12 +204,6 @@
                     moments[sites, :] = weighted
                 else:
                     moments[sites, :] += weighted
-        stores.append(
-            pltpu.make_async_copy(
-                outs[i], cheb_ref.at[c, :, :, pl.ds(k * LANES, LANES)], store_sem.at[i]
-            )
-        )
-        stores[i].start()
         if c == 0 and k == halves - 1:
             ones = jnp.ones((8, LANES), jnp.float32)
             gvalue = lax.dot_general(
@@ -247,8 +243,6 @@
             copy.wait_send()
     for copy in term_copies:
         copy.wait_send()
-    for copy in stores:
-        copy.wait()
 
 
 def on_device(n_rows, n_patch, panel, pairing, hop_blocks, hop_cols, bnd_weight, attract, attract_class, target):
@@ -260,7 +254,7 @@
     n_peers = n_rows // 2 - 1
     dma = pltpu.SemaphoreType.DMA
     vmem = pl.BlockSpec(memory_space=pltpu.VMEM)
-    anywhere = pl.BlockSpec(memory_space=pl.ANY)
+    in_hbm = pl.BlockSpec(memory_space=pltpu.HBM)
 
     blocks = rows // BLOCK
 
@@ -270,18 +264,17 @@
     cheb_two, new_pair, class_grad = pl.pallas_call(
         functools.partial(kernel, n_rows, n_patch),
         out_shape=(
-            jax.ShapeDtypeStruct((2, blocks, BLOCK, width), jnp.bfloat16),
-            jax.ShapeDtypeStruct((1, rows), jnp.float32),
-            jax.ShapeDtypeStruct((1, classes // n_rows), jnp.float32),
+            pltpu.VMEM((2, blocks, BLOCK, width), jnp.bfloat16),
+            pltpu.VMEM((1, rows), jnp.float32),
+            pltpu.VMEM((1, classes // n_rows), jnp.float32),
         ),
-        in_specs=[pl.BlockSpec(memory_space=pltpu.SMEM)] + [vmem] * 5 + [anywhere] * 2,
-        out_specs=(anywhere, vmem, vmem),
+        in_specs=[pl.BlockSpec(memory_space=pltpu.SMEM)] + [vmem, in_hbm] + [vmem] * 3 + [in_hbm] * 2,
+        out_specs=(vmem, vmem, vmem),
         scratch_shapes=[
             each(n_rows * blocks),
             each(n_rows * blocks),
             each(n_near * edge // BLOCK),
             each(n_near * edge // BLOCK),
-            each(blocks),
             pltpu.VMEM(hop_blocks.shape, jnp.bfloat16),
             pltpu.VMEM((rows, LANES), jnp.float32),
             pltpu.VMEM((rows, LANES), jnp.float32),
@@ -298,7 +291,8 @@
             dma((n_rows - 1,)),
             dma((n_chunks,)),
             dma,
-            dma((n_chunks,)),
+            pltpu.VMEM(bnd_weight.shape, jnp.bfloat16),
+            dma,
         ],
         compiler_params=pltpu.CompilerParams(
             collective_id=0, has_side_effects=True, vmem_limit_bytes=56 * 1024 * 1024

time: 38.2 us -> 36 us (0.942)
  Pallas kernels: 34.4 us -> 33.3 us
  local copies, waits for them, and re-layouts: 2.98 us -> 1.88 us
    pallas_call x1, Pallas kernels: 34.4 us -> 33.3 us  [on_device(): pl.pallas_call(functools.partial(kernel, n_rows, n_patch), out_shape=(plt...]
    unnamed x7 -> x3, local copies, waits for them, and re-layouts: 2.98 us -> 1.88 us
where the time goes in v2:
time: 36 us; the launch traced here: 35.8 us
  Pallas kernels  33.3 us (92%)
  local copies, waits for them, and re-layouts  1.88 us (5%)
  between operations  0.64 us (2%)
    pallas_call x1, Pallas kernels, on_device(): pl.pallas_call(functools.partial(kernel, n_rows, n_patch), out_shape=(plt...  33.3 us
    unnamed x3, local copies, waits for them, and re-layouts  1.88 us

profile of v2, /device:TPU:0, one launch (start us, length us, event | category | flops | bytes accessed | tf_op | source)
XLA Modules:
  0.0 35.8 jit_solution(12626300939470075673)
XLA Ops:
  0.6 33.3 %shard_map.103 = (bf16[2,4,128,256]{3,2,1,0:T(8,128)(2,1)S(1)}, f32[1,512]{1,0:T(1,128)S(1)}, f32[1,16]{1,0:T(1,128)S(1)}) custom-call(s32[4,8]{1,0:T(4,128)} %cols_ref.1, f32[1,512]{1,0:T(1,128)} %bitcast.10, bf16[128,512]{1,0:T(8,128)(2,1)} %bnd_hbm.1, f32[1,64]{1,0:T(1,128)} %bitcast.13, s32[1,512]{1,0:T(1,128)} %bitcast.11, f32[1,512]{1,0:T(1,128)} %bitcast.12, ...), custom_call_target="tpu_custom_call" | custom-call | tf_op jit(solution)/shard_map/pallas_call | solution.py:264
  33.9 0.8 %copy.14 = bf16[2,512,256]{2,1,0:T(8,128)(2,1)} copy(bf16[2,512,256]{2,1,0:T(8,128)(2,1)S(1)} %bitcast.7) | data formatting | bytes 1048576
  34.7 0.6 %copy.15 = f32[512]{0:T(512)} copy(f32[512]{0:T(512)S(1)} %bitcast.8) | data formatting | bytes 4096
  35.3 0.5 %copy.16 = f32[1,16]{1,0:T(1,128)} copy(f32[1,16]{1,0:T(1,128)S(1)} %get-tuple-element.11) | data formatting | bytes 128

commit v3 on v2

--- a/solution.py
+++ b/solution.py
@@ -30,7 +30,7 @@
 def kernel(
     n_rows, n_patch,
     cols_ref, pairing_ref, bnd_hbm, attract_ref, class_ref, target_ref, panel_ref, hop_ref,
-    cheb_ref, pair_out_ref, grad_ref,
+    cheb_ref, small_ref,
     pbufs, fbufs, pnear, fnear, hop, pair, moments, terms,
     peer_send, peer_recv, mate_send, mate_recv, fwd_send, fwd_recv,
     near_send, near_recv, term_send, term_recv, load_sem, hop_sem, bnd_ref, bnd_sem,
@@ -146,7 +146,11 @@
         started.append(
             sends(i, panel_ref.at[c, :, :, lanes], panel_ref.at[c, pl.ds(0, edge_blocks), :, lanes], pbufs[i], pnear[i])
         )
-        launch(started[i])
+        for copy in started[i][0]:
+            copy.start()
+    for _, to_mate, to_near, _ in started:
+        for copy in to_near + [to_mate]:
+            copy.start()
 
     for b in range(rows // BLOCK):
         sites = pl.ds(b * BLOCK, BLOCK)
@@ -182,7 +186,24 @@
         )
         for d in range(1, n_rows)
     ]
+    def add_terms():
+        for copy in term_copies:
+            copy.wait_recv()
+        total = terms[0]
+        for d in range(1, n_rows):
+            total = total + terms[d]
+        share = classes // n_rows
+        pick = (
+            lax.broadcasted_iota(jnp.int32, (classes, share), 0)
+            == lax.broadcasted_iota(jnp.int32, (classes, share), 1) + me * share
+        ).astype(jnp.float32)
+        small_ref[:, pl.ds(rows, share)] = jnp.dot(
+            total, pick, precision=HIGHEST, preferred_element_type=jnp.float32
+        )[:1]
+
     for i, (c, k) in enumerate(chunks):
+        if i == n_chunks - 1:
+            add_terms()
         arrive(started[n_chunks + i])
         other = (1 - c) * halves + k
         for b in range(rows // BLOCK):
@@ -216,27 +237,13 @@
                 jnp.broadcast_to(attract_ref[...], (8, classes)), onehot, precision=HIGHEST,
                 preferred_element_type=jnp.float32,
             )
-            pair_out_ref[...] = (gain * gvalue)[:1]
+            small_ref[:, pl.ds(0, rows)] = (gain * gvalue)[:1]
             terms[0] = lax.dot_general(
                 target_ref[...] * gvalue, onehot, LANE_DIMS, precision=HIGHEST,
                 preferred_element_type=jnp.float32,
             )
             for copy in term_copies:
                 copy.start()
-
-    for copy in term_copies:
-        copy.wait_recv()
-    total = terms[0]
-    for d in range(1, n_rows):
-        total = total + terms[d]
-    share = classes // n_rows
-    pick = (
-        lax.broadcasted_iota(jnp.int32, (classes, share), 0)
-        == lax.broadcasted_iota(jnp.int32, (classes, share), 1) + me * share
-    ).astype(jnp.float32)
-    grad_ref[...] = jnp.dot(
-        total, pick, precision=HIGHEST, preferred_element_type=jnp.float32
-    )[:1]
 
     for peers, to_mate, to_near, forwards in started:
         for copy in peers + [to_mate] + to_near + forwards:
@@ -261,15 +268,14 @@
     def each(count):
         return [pltpu.VMEM((count, BLOCK, LANES), jnp.bfloat16) for _ in range(n_chunks)]
 
-    cheb_two, new_pair, class_grad = pl.pallas_call(
+    cheb_two, small = pl.pallas_call(
         functools.partial(kernel, n_rows, n_patch),
         out_shape=(
             pltpu.VMEM((2, blocks, BLOCK, width), jnp.bfloat16),
-            pltpu.VMEM((1, rows), jnp.float32),
-            pltpu.VMEM((1, classes // n_rows), jnp.float32),
+            pltpu.VMEM((1, rows + classes // n_rows), jnp.float32),
         ),
         in_specs=[pl.BlockSpec(memory_space=pltpu.SMEM)] + [vmem, in_hbm] + [vmem] * 3 + [in_hbm] * 2,
-        out_specs=(vmem, vmem, vmem),
+        out_specs=(vmem, vmem),
         scratch_shapes=[
             each(n_rows * blocks),
             each(n_rows * blocks),
@@ -302,7 +308,7 @@
         attract_class.reshape(1, rows), target.reshape(1, rows),
         panel.reshape(2, blocks, BLOCK, width), hop_blocks,
     )
-    return cheb_two.reshape(panel.shape), new_pair.reshape(rows), class_grad
+    return cheb_two.reshape(panel.shape), small[0, :rows], small[:, rows:]
 
 
 def solution(mesh):

time: 36 us -> 36 us (level)
    slice x0 -> x2, local copies, waits for them, and re-layouts: none -> 1.09 us  [on_device(): return (cheb_two.reshape(panel.shape), small[0, :rows], small[:, rows:])]
    unnamed x3 -> x1, local copies, waits for them, and re-layouts: 1.88 us -> 0.8 us
where the time goes in v3:
time: 36 us; the launch traced here: 35.8 us
  Pallas kernels  33.3 us (92%)
  local copies, waits for them, and re-layouts  1.89 us (5%)
  between operations  0.64 us (2%)
    pallas_call x1, Pallas kernels, on_device(): pl.pallas_call(functools.partial(kernel, n_rows, n_patch), out_shape=(plt...  33.3 us
    slice x2, local copies, waits for them, and re-layouts, on_device(): return (cheb_two.reshape(panel.shape), small[0, :rows], small[:, rows:])  1.09 us
    unnamed x1, local copies, waits for them, and re-layouts  0.8 us

profile of v3, /device:TPU:0, one launch (start us, length us, event | category | flops | bytes accessed | tf_op | source)
XLA Modules:
  0.0 35.8 jit_solution(4558008271481646798)
XLA Ops:
  0.6 33.3 %shard_map.103 = (bf16[2,4,128,256]{3,2,1,0:T(8,128)(2,1)S(1)}, f32[1,528]{1,0:T(1,128)S(1)}) custom-call(s32[4,8]{1,0:T(4,128)} %cols_ref.1, f32[1,512]{1,0:T(1,128)} %bitcast.9, bf16[128,512]{1,0:T(8,128)(2,1)} %bnd_hbm.1, f32[1,64]{1,0:T(1,128)} %bitcast.13, s32[1,512]{1,0:T(1,128)} %bitcast.10, f32[1,512]{1,0:T(1,128)} %bitcast.11, ...), custom_call_target="tpu_custom_call" | custom-call | tf_op jit(solution)/shard_map/pallas_call | solution.py:271
  33.9 0.8 %copy.12 = bf16[2,512,256]{2,1,0:T(8,128)(2,1)} copy(bf16[2,512,256]{2,1,0:T(8,128)(2,1)S(1)} %bitcast.7) | data formatting | bytes 1048576
  34.7 0.5 %slice.7 = f32[1,16]{1,0:T(1,128)} slice(f32[1,528]{1,0:T(1,128)S(1)} %get-tuple-element.6), slice={[0:1], [512:528]} | slice | bytes 128 | tf_op jit(solution)/shard_map/slice | solution.py:311
  35.2 0.6 %slice.6 = f32[1,512]{1,0:T(1,128)} slice(f32[1,528]{1,0:T(1,128)S(1)} %get-tuple-element.6), slice={[0:1], [0:512]} | slice | bytes 4096 | tf_op jit(solution)/shard_map/slice | solution.py:311
